TPU v7x, 256 devices: a whole 4x4x8 slice. The times are simulated.
256 devices in a mesh: row: 32 (over y, x, core), col: 8 (over z).
Axes of the slice: x: 4, y: 4, z: 8, core: 2. Of those that a mesh axis runs over, the one named last changes fastest.
Arguments:
- gram: float32 [16384, 16384], P('row', 'col'), may hold values from -70 to 70, as said below
- descriptors: float32 [16384, 2048], P('row', 'col'), may hold values from -0.6 to 0.6
Outputs:
- factored: float32 [16384, 16384], P('row', 'col')
- reduced: float32 [16384, 2048], P('row', 'col')
- variance: float32 [2048], P('col')
Inputs may be any that keep to these rules, and one draw needn't show every extreme that they name: `gram`: symmetric positive definite in natural order with a positive diagonal; columns stored as the steps say.
All inputs are finite; a program needn't handle non-finite values.
Results may differ from a plain program's by a relative error of at most 0.0001.
Values sent between devices are 32-bit elements; how exact they have to be, the bound alone decides.
No kernel may reach another device: no remote copies, remote signals or barrier semaphores. Data moves between devices by JAX's collectives and lax.ppermute only.
A program may use at most 128 MiB of HBM per device.

v0:
```python
import functools

import jax
import jax.numpy as jnp
from jax import lax
from jax.experimental import pallas as pl
from jax.experimental.pallas import tpu as pltpu
from jax.sharding import PartitionSpec as P

HIGHEST = lax.Precision.HIGHEST
TILE = 128
SUB = 8


def lane_of(x, at):
    return jnp.broadcast_to(x[:, at:at + 1], x.shape)


def sub_of(x, at):
    return jnp.broadcast_to(x[at:at + 1, :], x.shape)


def invert_tile(rows):
    shape = rows[0].shape
    lane = lax.broadcasted_iota(jnp.int32, shape, 1)
    sub = lax.broadcasted_iota(jnp.int32, shape, 0)
    count = len(rows)
    for p in range(count):
        at = SUB * p
        panel = (lane >= at) & (lane < at + SUB)
        row = rows[p]
        diag = [lane_of(row, at + k) for k in range(SUB)]
        row = jnp.where(panel, jnp.where(lane == sub + at, 1.0, 0.0), row)
        inv, tops, low = [], [], {}
        for k in range(SUB):
            scale = lax.rsqrt(sub_of(diag[k], k))
            inv.append(scale)
            mult = diag[k] * scale
            top = sub_of(row, k) * scale
            tops.append(top)
            for j in range(k + 1, SUB):
                low[j, k] = sub_of(diag[j], k) * scale
                diag[j] = diag[j] - mult * low[j, k]
            row = row - mult * top
        done = tops[0]
        for k in range(1, SUB):
            done = jnp.where(sub == k, tops[k], done)
        rows[p] = jnp.where(lane <= sub + at, done, 0.0)
        for i in range(p + 1, count):
            cols = [lane_of(rows[i], at + k) for k in range(SUB)]
            rest = jnp.where(panel, 0.0, rows[i])
            for k in range(SUB):
                mult = cols[k] * inv[k]
                for j in range(k + 1, SUB):
                    cols[j] = cols[j] - mult * low[j, k]
                rest = rest - mult * tops[k]
            rows[i] = rest
    return jnp.concatenate(rows, axis=0)


def block(i):
    return pl.ds(pl.multiple_of(i * TILE, TILE), TILE)


def factor_in_place(t_ref):
    count = t_ref.shape[0] // TILE

    def step(j, carry):
        here = block(j)
        rows = [
            t_ref[pl.ds(pl.multiple_of(j * TILE + SUB * i, SUB), SUB), here]
            for i in range(TILE // SUB)
        ]
        tile = invert_tile(rows)
        t_ref[here, :] = jnp.dot(tile, t_ref[here, :], precision=HIGHEST)
        t_ref[here, here] = tile

        def below(i, carry):
            there = block(i)
            left = t_ref[here, there]
            t_ref[there, here] = jnp.zeros((TILE, TILE), jnp.float32)
            t_ref[there, :] -= lax.dot_general(
                left, t_ref[here, :], (((0,), (0,)), ((), ())), precision=HIGHEST,
                preferred_element_type=jnp.float32,
            )
            return carry

        return lax.fori_loop(j + 1, count, below, carry)

    lax.fori_loop(0, count, step, 0)


def mask_lower(t_ref):
    order = t_ref.shape[0]
    for j in range(order // TILE - 1):
        t_ref[j * TILE:(j + 1) * TILE, (j + 1) * TILE:] = jnp.zeros(
            (TILE, order - (j + 1) * TILE), jnp.float32
        )


def split(x):
    high = x.astype(jnp.bfloat16)
    return high, (x - high.astype(jnp.float32)).astype(jnp.bfloat16)


def dot3(left, right, dims):
    def one(x, y):
        return lax.dot_general(x, y, (dims, ((), ())), preferred_element_type=jnp.float32)
    return one(left[0], right[1]) + one(left[1], right[0]) + one(left[0], right[0])


NN = ((1,), (0,))
NT = ((1,), (1,))


def tile_home(q, c, core, nb, ncol):
    slab = nb // ncol
    pairs = nb // TILE // 2
    row = c * slab + (q // pairs) * SUB
    col = (q % pairs) * 2 * TILE + core * TILE
    return slice(row, row + SUB), pl.ds(pl.multiple_of(col, TILE), TILE)


def first_kernel(core_ref, own_ref, other_ref, t_ref):
    core = core_ref[0]
    nb = t_ref.shape[0]
    count, ncol = own_ref.shape[:2]
    for q in range(count):
        for c in range(ncol):
            t_ref[tile_home(q, c, core, nb, ncol)] = own_ref[q, c]
            t_ref[tile_home(q, c, 1 - core, nb, ncol)] = other_ref[q, c]
    factor_in_place(t_ref)
    mask_lower(t_ref)


def second_kernel(at_ref, own_ref, other_ref, first_ref, mine_ref, desc_ref,
                  panel_ref, high_ref, low_ref, reduced_ref, var_ref,
                  left_ref, t_ref, x_ref):
    core, prow, pcol = at_ref[0], at_ref[1], at_ref[2]
    nb = t_ref.shape[0]
    qn = x_ref.shape[1]
    count = own_ref.shape[0]
    ncol = nb // SUB // SUB
    for q in range(count):
        for c in range(ncol):
            here = tile_home(q, c, core, nb, ncol)
            there = tile_home(q, c, 1 - core, nb, ncol)
            left_ref[here] = own_ref[q, 2 * c]
            left_ref[there] = other_ref[q, 2 * c]
            t_ref[here] = own_ref[q, 2 * c + 1]
            t_ref[there] = other_ref[q, 2 * c + 1]
        chunk = nb // count // 2
        for t in range(own_ref.shape[1] - 2 * ncol):
            part, tile = divmod(t, chunk // SUB * (qn // TILE))
            row = part * nb + 2 * q * chunk + tile // (qn // TILE) * SUB
            cols = slice(tile % (qn // TILE) * TILE, (tile % (qn // TILE) + 1) * TILE)
            here = pl.ds(pl.multiple_of(row + core * chunk, SUB), SUB)
            there = pl.ds(pl.multiple_of(row + (1 - core) * chunk, SUB), SUB)
            x_ref[here, cols] = own_ref[q, 2 * ncol + t]
            x_ref[there, cols] = other_ref[q, 2 * ncol + t]
    first = first_ref[...]
    left = lax.dot_general(
        left_ref[...], first, (NT, ((), ())), precision=HIGHEST,
        preferred_element_type=jnp.float32,
    )
    left_ref[...] = left
    t_ref[...] -= lax.dot_general(
        left, left, (NT, ((), ())), precision=HIGHEST, preferred_element_type=jnp.float32,
    )
    factor_in_place(t_ref)
    mask_lower(t_ref)
    left_ref[...] = jnp.dot(left_ref[...], first_ref[...], precision=HIGHEST)
    left_ref[...] = -jnp.dot(t_ref[...], left_ref[...], precision=HIGHEST)

    l00 = split(first_ref[...])
    l10 = split(left_ref[...])
    l11 = split(t_ref[...])
    m0 = split(mine_ref[:, :nb])
    m1 = split(mine_ref[:, nb:])
    p0 = dot3(m0, l00, NT)
    p1 = dot3(m0, l10, NT) + dot3(m1, l11, NT)
    row = prow * nb + lax.broadcasted_iota(jnp.int32, (nb, nb), 0)
    col = pcol * nb + lax.broadcasted_iota(jnp.int32, (nb, nb), 1)
    panel_ref[...] = jnp.where(row >= col, jnp.where(pcol == 0, p0, p1), 0.0)
    p0, p1 = split(p0), split(p1)
    w0 = split(dot3(p0, l00, NN) + dot3(p1, l10, NN))
    w1 = split(dot3(p1, l11, NN))
    high_ref[:, :nb] = w0[0]
    low_ref[:, :nb] = w0[1]
    high_ref[:, nb:] = w1[0]
    low_ref[:, nb:] = w1[1]
    x0 = split(x_ref[:nb])
    x1 = split(x_ref[nb:])
    z0 = dot3(l00, x0, NN)
    z1 = dot3(l10, x0, NN) + dot3(l11, x1, NN)
    var_ref[...] = jnp.sum(z0 * z0, axis=0, keepdims=True) + jnp.sum(z1 * z1, axis=0, keepdims=True)
    lowered = desc_ref[...] - (dot3(w0, x0, NN) + dot3(w1, x1, NN))
    reduced_ref[...] = jnp.where(prow == 0, z0, jnp.where(prow == 1, z1, lowered))


VMEM = pl.BlockSpec(memory_space=pltpu.VMEM)
SMEM = pl.BlockSpec(memory_space=pltpu.SMEM)


def factor_first(core, own, other, nb):
    return pl.pallas_call(
        first_kernel,
        out_shape=jax.ShapeDtypeStruct((nb, nb), jnp.float32),
        in_specs=[SMEM, VMEM, VMEM],
        out_specs=VMEM,
        compiler_params=pltpu.CompilerParams(vmem_limit_bytes=24 * 2**20),
        cost_estimate=pl.CostEstimate(flops=150 * nb**3, bytes_accessed=8 * nb * nb, transcendentals=0),
        name="factor_first",
    )(core, own, other)


def factor_second(at, own, other, first, mine, desc):
    nb, order = mine.shape
    qn = desc.shape[1]
    return pl.pallas_call(
        second_kernel,
        out_shape=(
            jax.ShapeDtypeStruct((nb, nb), jnp.float32),
            jax.ShapeDtypeStruct((nb, order), jnp.bfloat16),
            jax.ShapeDtypeStruct((nb, order), jnp.bfloat16),
            jax.ShapeDtypeStruct((nb, qn), jnp.float32),
            jax.ShapeDtypeStruct((1, qn), jnp.float32),
        ),
        in_specs=[SMEM] + [VMEM] * 5,
        out_specs=(VMEM,) * 5,
        scratch_shapes=[pltpu.VMEM((nb, nb), jnp.float32)] * 2 + [pltpu.VMEM((order, qn), jnp.float32)],
        compiler_params=pltpu.CompilerParams(vmem_limit_bytes=60 * 2**20),
        cost_estimate=pl.CostEstimate(flops=300 * nb**3, bytes_accessed=40 * nb * nb, transcendentals=0),
        name="factor_second",
    )(at, own, other, first, mine, desc)


WIDTH = 256


def update_kernel(flip, at_ref, gram_ref, match_ref, high_ref, low_ref, panel_ref, *refs):
    out_ref = refs[-1]
    prow, pcol = at_ref[1], at_ref[2]
    nb = gram_ref.shape[0]
    steps = pl.num_programs(0)
    half = at_ref[0] if not flip else 1 - at_ref[0]
    tile = half * steps + pl.program_id(0)
    is_panel = (pcol < 2) & (tile < nb // WIDTH)

    @pl.when(is_panel)
    def _():
        out_ref[...] = panel_ref[:, pl.ds(pl.multiple_of(tile * WIDTH, WIDTH), WIDTH)]

    @pl.when(jnp.logical_not(is_panel) & (prow < 2))
    def _():
        out_ref[...] = jnp.zeros((nb, WIDTH), jnp.float32)

    @pl.when(jnp.logical_not(is_panel) & (prow >= 2))
    def _():
        match = split(match_ref[...])
        out_ref[...] = gram_ref[...] - dot3((high_ref[...], low_ref[...]), match, NT)


def update(at, gram, match, high, low, panel, done=None):
    nb, stored = gram.shape
    order = high.shape[1]
    steps = stored // 2 // WIDTH
    flip = done is not None

    def place(t, at_ref):
        half = 1 - at_ref[0] if flip else at_ref[0]
        return (0, half * steps + t)

    whole = pl.BlockSpec((nb, order), lambda t, at_ref: (0, 0))
    in_specs = [
        pl.BlockSpec((nb, WIDTH), place),
        pl.BlockSpec((WIDTH, order), lambda t, at_ref: (t, 0)),
        whole, whole, pl.BlockSpec((nb, nb), lambda t, at_ref: (0, 0)),
    ]
    args = [gram, match, high, low, panel]
    if flip:
        in_specs.append(pl.BlockSpec(memory_space=pl.ANY))
        args.append(done)
    return pl.pallas_call(
        functools.partial(update_kernel, flip),
        grid_spec=pltpu.PrefetchScalarGridSpec(
            num_scalar_prefetch=1,
            grid=(steps,),
            in_specs=in_specs,
            out_specs=pl.BlockSpec((nb, WIDTH), place),
        ),
        out_shape=jax.ShapeDtypeStruct((nb, stored), jnp.float32),
        input_output_aliases={6: 0} if flip else {},
        compiler_params=pltpu.CompilerParams(vmem_limit_bytes=60 * 2**20),
        cost_estimate=pl.CostEstimate(
            flops=6 * nb * stored * order // 2, bytes_accessed=4 * nb * stored + 2 * stored * order,
            transcendentals=0,
        ),
        name="update_other" if flip else "update_own",
    )(at, *args)


def spread(x, axis, groups=None):
    size = lax.axis_size(axis) if groups is None else len(groups[0])
    return lax.all_to_all(
        jnp.broadcast_to(x[None], (size,) + x.shape), axis, 0, 0, tiled=True,
        axis_index_groups=groups,
    )


def body(gram, desc):
    nb = gram.shape[0]
    qn = desc.shape[1]
    nrow, ncol = lax.axis_size("row"), lax.axis_size("col")
    groups = nrow // ncol
    order = 2 * nb
    prow = lax.axis_index("row")
    pcol = lax.axis_index("col")
    core = prow % 2
    slab = nb // ncol
    wide = nb // TILE
    lanes = [[2 * q + k for q in range(nrow // 2)] for k in range(2)]
    swap = [(r, r ^ 1) for r in range(nrow)]
    front = gram[:, :nb]

    chunk = nb // nrow
    heads = desc.reshape(nrow, chunk // SUB, SUB, qn // TILE, TILE).transpose(0, 1, 3, 2, 4)
    heads = heads.reshape(nrow, -1, SUB, TILE)
    heads = lax.all_to_all(heads, "row", 0, 0, tiled=True)

    front = front.reshape(ncol, slab, nb)
    slab0 = jnp.where(pcol == 0, front[0], 0.0)
    slab1 = jnp.where(pcol == 1, front[1], 0.0)
    for s in range(1, ncol):
        piece = jnp.where(pcol == 0, front[s], front[(s + 1) % ncol])
        come = lax.ppermute(piece, "col", [(0, s), (1, (s + 1) % ncol)])
        slab0 = jnp.where(pcol == s, come, slab0)
        slab1 = jnp.where(pcol == (s + 1) % ncol, come, slab1)
    heads, slab0, slab1 = lax.optimization_barrier((heads, slab0, slab1))
    rows_slab = jnp.concatenate([slab0, slab1], axis=1)

    mine = lax.all_gather(rows_slab, "col", tiled=True)

    tiles = rows_slab.reshape(slab // SUB, SUB, 2, wide, TILE).transpose(0, 3, 2, 1, 4)
    tiles = tiles.reshape(nrow, 2, SUB, TILE)
    dealt = lax.all_to_all(tiles, "row", 0, 0, tiled=True)

    half = groups // 2
    pairs = []
    for y in range(groups):
        for i in range(ncol):
            for c in range(ncol):
                to = 2 * ((y % half) * ncol + c) + y // half
                pairs.append(((y * ncol + i) * ncol + c, to * ncol + i))
    match = lax.ppermute(rows_slab, ("row", "col"), pairs)

    lead = spread(jnp.concatenate([dealt[0, :1], dealt[1]], axis=0), "col")

    match, lead = lax.optimization_barrier((match, lead))
    lead_own = spread(lead[:, 0], "row", lanes)
    match = lax.all_gather(match, "row", axis_index_groups=lanes, tiled=True)
    lead_other = lax.ppermute(lead_own, "row", swap)
    following = jnp.concatenate(
        [lead[:, 1:].reshape(2 * ncol, SUB, TILE), heads[0], heads[1]], axis=0
    )
    next_own = spread(following, "row", lanes)
    lead_own, mine = lax.optimization_barrier((lead_own, mine))
    index = jnp.stack([core, prow, pcol]).astype(jnp.int32)
    first = factor_first(index, lead_own, lead_other, nb)

    first, next_own = lax.optimization_barrier((first, next_own))
    next_other = lax.ppermute(next_own, "row", swap)
    panel, high, low, reduced, variance = factor_second(
        index, next_own, next_other, first, mine, desc
    )

    high, match = lax.optimization_barrier((high, match))
    other = lax.ppermute(match, "row", swap)
    rest = update(index, gram, match, high, low, panel)
    rest = update(index, gram, other, high, low, panel, rest)
    return (rest, reduced, variance.reshape(qn))


def solution(mesh):
    in_specs = (P("row", "col"), P("row", "col"))
    out_specs = (P("row", "col"), P("row", "col"), P("col"))
    return jax.shard_map(body, mesh=mesh, in_specs=in_specs, out_specs=out_specs, check_vma=False)
```

profile of v0, /device:TPU:9, one launch (start us, length us, event | category | flops | bytes accessed | tf_op | source)
XLA Modules:
  0.0 207.1 jit_solution(12427829419001729505)
XLA Ops:
  7.2 1.4 slice_select_fusion
  8.6 7.5 %collective-permute-start = (f32[64,512]{1,0:T(8,128)S(1)}, f32[64,512]{1,0:T(8,128)S(1)}, u32[]{:S(2)}, u32[]{:S(2)}) collective-permute-start(f32[64,512]{1,0:T(8,128)S(1)} %get-tuple-element.43), channel_id=1, source_target_pairs={{0,7},{1,0},{8,15},{9,8},{16,23},{17,16},{24,31},{25,24},{32,39},{... | collective-permute-start | bytes 393224 | tf_op jit(solution)/shard_map/ppermute | solution.py:336
  16.1 1.3 collective-permute-start.1
  17.4 8.1 %all-to-all-start = ((f32[32,4,8,128]{3,2,1,0:T(8,128)}), f32[32,4,8,128]{3,2,1,0:T(8,128)S(1)}, u32[]{:S(2)}, u32[]{:S(2)}) async-start(f32[32,4,8,128]{3,2,1,0:T(8,128)} %bitcast.25), calls=%async_computation | async-start | bytes 1048576 | tf_op jit(solution)/shard_map/all_to_all | solution.py:329
  25.5 0.0 all-gather.3.cloned.1.call-start
  25.6 1.3 collective-permute-start.2
  26.9 1.3 collective-permute-start.3
  28.2 1.3 collective-permute-start.4
  29.5 0.0 collective-permute-done
  29.5 1.3 collective-permute-start.5
  30.8 0.0 collective-permute-done.1
  30.8 3.1 %collective-permute-start.6 = (f32[64,512]{1,0:T(8,128)S(1)}, f32[64,512]{1,0:T(8,128)S(1)}, u32[]{:S(2)}, u32[]{:S(2)}) collective-permute-start(f32[64,512]{1,0:T(8,128)S(1)} %get-tuple-element.37), channel_id=1, source_target_pairs={{0,1},{1,2},{8,9},{9,10},{16,17},{17,18},{24,25},{25,26},{32,33},{... | collective-permute-start | bytes 393224 | tf_op jit(solution)/shard_map/ppermute | solution.py:336
  33.9 1.2 collective-permute-done.2
  35.2 0.0 collective-permute-done.3
  35.2 0.0 collective-permute-done.4
  35.2 1.5 collective-permute-done.5
  36.7 2.8 %collective-permute-done.6 = f32[64,512]{1,0:T(8,128)S(1)} collective-permute-done((f32[64,512]{1,0:T(8,128)S(1)}, f32[64,512]{1,0:T(8,128)S(1)}, u32[]{:S(2)}, u32[]{:S(2)}) %collective-permute-start.6) | collective-permute-done | bytes 131104 | tf_op jit(solution)/shard_map/ppermute | solution.py:336
  39.5 1.1 select_select_fusion
  40.6 0.0 all-to-all-done
  40.6 0.0 copy-start.2
  40.6 0.7 copy-done.2
  41.3 0.0 all-gather.3.cloned.1.call-update
  41.3 1.7 copy.9
  43.0 7.9 %all-to-all-start.1 = ((f32[32,2,8,128]{3,2,1,0:T(8,128)}), f32[32,2,8,128]{3,2,1,0:T(8,128)S(1)}, u32[]{:S(2)}, u32[]{:S(2)}) async-start(f32[32,2,8,128]{3,2,1,0:T(8,128)} %bitcast.8), calls=%async_computation.1 | async-start | bytes 524288 | tf_op jit(solution)/shard_map/all_to_all | solution.py:346
  50.9 9.8 %collective-permute-start.7 = (f32[64,1024]{1,0:T(8,128)}, f32[64,1024]{1,0:T(8,128)S(1)}, u32[]{:S(2)}, u32[]{:S(2)}) collective-permute-start(f32[64,1024]{1,0:T(8,128)} %copy-done.2), channel_id=1, source_target_pairs={{0,0},{1,16},{2,32},{3,48},{4,64},{5,80},{6,96},{7,112},{8,1},{9,1... | collective-permute-start | bytes 786440 | tf_op jit(solution)/shard_map/ppermute | solution.py:355
  60.8 0.0 all-to-all-done.1
  60.8 0.6 broadcast_in_dim.25
  61.4 7.9 %all-to-all-start.2 = ((f32[8,3,8,128]{3,2,1,0:T(8,128)}), f32[8,3,8,128]{3,2,1,0:T(8,128)S(1)}, u32[]{:S(2)}, u32[]{:S(2)}) async-start(f32[8,3,8,128]{3,2,1,0:T(8,128)} %broadcast_in_dim.25), calls=%async_computation.2 | async-start | bytes 196608 | tf_op jit(solution)/shard_map/all_to_all | solution.py:305
  69.4 0.0 collective-permute-done.7
  69.4 0.0 copy-start.4
  69.4 19.3 %all-to-all-done.2 = f32[8,3,8,128]{3,2,1,0:T(8,128)S(1)} async-done(((f32[8,3,8,128]{3,2,1,0:T(8,128)}), f32[8,3,8,128]{3,2,1,0:T(8,128)S(1)}, u32[]{:S(2)}, u32[]{:S(2)}) %all-to-all-start.2) | async-done | bytes 98336 | tf_op jit(solution)/shard_map/all_to_all | solution.py:305
  88.7 0.8 broadcast_in_dim.27
  89.5 4.7 %all-to-all-start.3 = ((f32[16,8,8,128]{3,2,1,0:T(8,128)}), f32[16,8,8,128]{3,2,1,0:T(8,128)S(1)}, u32[]{:S(2)}, u32[]{:S(2)}) async-start(f32[16,8,8,128]{3,2,1,0:T(8,128)} %broadcast_in_dim.27), calls=%async_computation.3 | async-start | bytes 1048576 | tf_op jit(solution)/shard_map/all_to_all | solution.py:305
  94.2 0.0 all-gather.5.cloned.1.call-start
  94.2 0.0 copy-done.4
  94.2 0.7 all-gather.5.cloned.1.call-update
  94.9 8.3 %all-to-all-done.3.own_ref = f32[16,8,8,128]{3,2,1,0:T(8,128)S(1)} async-done(((f32[16,8,8,128]{3,2,1,0:T(8,128)}), f32[16,8,8,128]{3,2,1,0:T(8,128)S(1)}, u32[]{:S(2)}, u32[]{:S(2)}) %all-to-all-start.3) | async-done | bytes 524320 | tf_op jit(solution)/shard_map/all_to_all | solution.py:305
  103.2 1.2 collective-permute-start.8
  104.4 0.1 pad_add_fusion.core_ref.at_ref
  104.4 0.0 copy-start
  104.5 1.3 broadcast_in_dim.28
  105.8 5.9 %all-to-all-start.4 = ((f32[16,24,8,128]{3,2,1,0:T(8,128)}), f32[16,24,8,128]{3,2,1,0:T(8,128)S(1)}, u32[]{:S(2)}, u32[]{:S(2)}) async-start(f32[16,24,8,128]{3,2,1,0:T(8,128)} %broadcast_in_dim.28), calls=%async_computation.4 | async-start | bytes 3145728 | tf_op jit(solution)/shard_map/all_to_all | solution.py:305
  111.7 0.0 all-gather.3.cloned.1.call-done.mine_ref
  111.7 0.0 collective-permute-done.8.other_ref
  111.7 20.4 %factor_first.1.first_ref = f32[512,512]{1,0:T(8,128)S(1)} custom-call(s32[3]{0:T(128)S(1)} %pad_add_fusion.core_ref.at_ref, f32[16,8,8,128]{3,2,1,0:T(8,128)S(1)} %all-to-all-done.3.own_ref, f32[16,8,8,128]{3,2,1,0:T(8,128)S(1)} %collective-permute-done.8.other_ref), custom_call_target="tpu_custom_call" | custom-call | flops 20132659200 | bytes 2097152 | tf_op jit(solution)/shard_map/factor_first/pallas_call | solution.py:206
  132.1 0.0 copy-done
  132.1 0.0 copy-start.1
  132.1 1.0 copy-done.1
  133.1 7.3 %all-to-all-done.4.own_ref = f32[16,24,8,128]{3,2,1,0:T(8,128)S(1)} async-done(((f32[16,24,8,128]{3,2,1,0:T(8,128)}), f32[16,24,8,128]{3,2,1,0:T(8,128)S(1)}, u32[]{:S(2)}, u32[]{:S(2)}) %all-to-all-start.4) | async-done | bytes 1572896 | tf_op jit(solution)/shard_map/all_to_all | solution.py:305
  140.4 0.0 copy-start.3
  140.4 0.8 collective-permute-start.9
  141.2 3.0 %collective-permute-done.9.other_ref = f32[16,24,8,128]{3,2,1,0:T(8,128)S(1)} collective-permute-done((f32[16,24,8,128]{3,2,1,0:T(8,128)S(1)}, f32[16,24,8,128]{3,2,1,0:T(8,128)S(1)}, u32[]{:S(2)}, u32[]{:S(2)}) %collective-permute-start.9) | collective-permute-done | bytes 1572896 | tf_op jit(solution)/shard_map/ppermute | solution.py:372
  144.3 0.0 copy-done.3
  144.3 0.0 copy-start.5
  144.3 1.1 copy-done.5
  145.4 37.9 %factor_second.1 = (f32[512,512]{1,0:T(8,128)}, bf16[512,1024]{1,0:T(8,128)(2,1)}, bf16[512,1024]{1,0:T(8,128)(2,1)}, f32[512,256]{1,0:T(8,128)}, f32[1,256]{1,0:T(1,128)}) custom-call(s32[3]{0:T(128)} %copy-done, f32[16,24,8,128]{3,2,1,0:T(8,128)} %copy-done.3, f32[16,24,8,128]{3,2,1,0:T(8,128)} %copy-done.5, f32[512,512]{1,0:T(8,128)} %copy-done.1, ...), custom_call_target="tpu_custom_call" | custom-call | flops 40265318400 | bytes 10485760 | tf_op jit(solution)/shard_map/factor_second/pallas_call | solution.py:220
  183.4 0.0 all-gather.5.cloned.1.call-done.match_ref
  183.4 0.4 collective-permute-start.10
  183.7 8.7 %update_own.1.refs_0_ = f32[512,2048]{1,0:T(8,128)} custom-call(s32[3]{0:T(128)} %copy-done, f32[512,2048]{1,0:T(8,128)} %gram_ref.3, f32[1024,1024]{1,0:T(8,128)} %all-gather.5.cloned.1.call-done.match_ref, bf16[512,1024]{1,0:T(8,128)(2,1)} %get-tuple-element.30.high_ref, bf16[512,1024]{1,0:T(8,128)(2,1)} %get-tuple-element.31.low_ref, ...), custom_call_target="tpu_custom_call" | custom-call | flops 3221225472 | bytes 8388608 | tf_op jit(solution)/shard_map/update_own/pallas_call | solution.py:284
  192.4 0.0 collective-permute-done.10.match_ref
  192.4 7.9 %update_other.1 = f32[512,2048]{1,0:T(8,128)} custom-call(s32[3]{0:T(128)} %copy-done, f32[512,2048]{1,0:T(8,128)} %gram_ref.3, f32[1024,1024]{1,0:T(8,128)} %collective-permute-done.10.match_ref, bf16[512,1024]{1,0:T(8,128)(2,1)} %get-tuple-element.30.high_ref, bf16[512,1024]{1,0:T(8,128)(2,1)} %get-tuple-element.31.low_ref, ...), custom_call_target="tpu_custom_call", output_to_operand_aliasing={{}: (6, {})} | custom-call | flops 3221225472 | bytes 8388608 | tf_op jit(solution)/shard_map/update_other/pallas_call | solution.py:284
  (9 shorter events, 0.1 us)
Async XLA Ops:
  8.6 20.9 %collective-permute-start = (f32[64,512]{1,0:T(8,128)S(1)}, f32[64,512]{1,0:T(8,128)S(1)}, u32[]{:S(2)}, u32[]{:S(2)}) collective-permute-start(f32[64,512]{1,0:T(8,128)S(1)} %get-tuple-element.43), channel_id=1, source_target_pairs={{0,7},{1,0},{8,15},{9,8},{16,23},{17,16},{24,31},{25,24},{32,39},{... | collective-permute-start | bytes 393224 | tf_op jit(solution)/shard_map/ppermute | solution.py:336
  16.1 14.7 %collective-permute-start.1 = (f32[64,512]{1,0:T(8,128)S(1)}, f32[64,512]{1,0:T(8,128)S(1)}, u32[]{:S(2)}, u32[]{:S(2)}) collective-permute-start(f32[64,512]{1,0:T(8,128)S(1)} %get-tuple-element.42), channel_id=1, source_target_pairs={{0,6},{1,7},{8,14},{9,15},{16,22},{17,23},{24,30},{25,31},{32,38},... | collective-permute-start | bytes 393224 | tf_op jit(solution)/shard_map/ppermute | solution.py:336
  17.4 23.2 %all-to-all-start = ((f32[32,4,8,128]{3,2,1,0:T(8,128)}), f32[32,4,8,128]{3,2,1,0:T(8,128)S(1)}, u32[]{:S(2)}, u32[]{:S(2)}) async-start(f32[32,4,8,128]{3,2,1,0:T(8,128)} %bitcast.25), calls=%async_computation | async-start | bytes 1048576 | tf_op jit(solution)/shard_map/all_to_all | solution.py:329
  25.5 86.2 %all-gather.3.cloned.1.call-start = ((), (), s32[]{:S(2)}) async-start(), calls=%async_computation.5 | async-start | bytes 2359296 | tf_op jit(solution)/shard_map/all_gather | solution.py:342
  25.6 9.6 %collective-permute-start.2 = (f32[64,512]{1,0:T(8,128)S(1)}, f32[64,512]{1,0:T(8,128)S(1)}, u32[]{:S(2)}, u32[]{:S(2)}) collective-permute-start(f32[64,512]{1,0:T(8,128)S(1)} %get-tuple-element.41), channel_id=1, source_target_pairs={{0,5},{1,6},{8,13},{9,14},{16,21},{17,22},{24,29},{25,30},{32,37},... | collective-permute-start | bytes 393224 | tf_op jit(solution)/shard_map/ppermute | solution.py:336
  26.9 8.3 %collective-permute-start.3 = (f32[64,512]{1,0:T(8,128)S(1)}, f32[64,512]{1,0:T(8,128)S(1)}, u32[]{:S(2)}, u32[]{:S(2)}) collective-permute-start(f32[64,512]{1,0:T(8,128)S(1)} %get-tuple-element.40), channel_id=1, source_target_pairs={{0,4},{1,5},{8,12},{9,13},{16,20},{17,21},{24,28},{25,29},{32,36},... | collective-permute-start | bytes 393224 | tf_op jit(solution)/shard_map/ppermute | solution.py:336
  28.2 7.0 %collective-permute-start.4 = (f32[64,512]{1,0:T(8,128)S(1)}, f32[64,512]{1,0:T(8,128)S(1)}, u32[]{:S(2)}, u32[]{:S(2)}) collective-permute-start(f32[64,512]{1,0:T(8,128)S(1)} %get-tuple-element.39), channel_id=1, source_target_pairs={{0,3},{1,4},{8,11},{9,12},{16,19},{17,20},{24,27},{25,28},{32,35},... | collective-permute-start | bytes 393224 | tf_op jit(solution)/shard_map/ppermute | solution.py:336
  29.5 7.2 %collective-permute-start.5 = (f32[64,512]{1,0:T(8,128)S(1)}, f32[64,512]{1,0:T(8,128)S(1)}, u32[]{:S(2)}, u32[]{:S(2)}) collective-permute-start(f32[64,512]{1,0:T(8,128)S(1)} %get-tuple-element.38), channel_id=1, source_target_pairs={{0,2},{1,3},{8,10},{9,11},{16,18},{17,19},{24,26},{25,27},{32,34},... | collective-permute-start | bytes 393224 | tf_op jit(solution)/shard_map/ppermute | solution.py:336
  30.8 8.7 %collective-permute-start.6 = (f32[64,512]{1,0:T(8,128)S(1)}, f32[64,512]{1,0:T(8,128)S(1)}, u32[]{:S(2)}, u32[]{:S(2)}) collective-permute-start(f32[64,512]{1,0:T(8,128)S(1)} %get-tuple-element.37), channel_id=1, source_target_pairs={{0,1},{1,2},{8,9},{9,10},{16,17},{17,18},{24,25},{25,26},{32,33},{... | collective-permute-start | bytes 393224 | tf_op jit(solution)/shard_map/ppermute | solution.py:336
  40.6 0.7 copy-start.2
  43.0 17.7 %all-to-all-start.1 = ((f32[32,2,8,128]{3,2,1,0:T(8,128)}), f32[32,2,8,128]{3,2,1,0:T(8,128)S(1)}, u32[]{:S(2)}, u32[]{:S(2)}) async-start(f32[32,2,8,128]{3,2,1,0:T(8,128)} %bitcast.8), calls=%async_computation.1 | async-start | bytes 524288 | tf_op jit(solution)/shard_map/all_to_all | solution.py:346
  50.9 18.5 %collective-permute-start.7 = (f32[64,1024]{1,0:T(8,128)}, f32[64,1024]{1,0:T(8,128)S(1)}, u32[]{:S(2)}, u32[]{:S(2)}) collective-permute-start(f32[64,1024]{1,0:T(8,128)} %copy-done.2), channel_id=1, source_target_pairs={{0,0},{1,16},{2,32},{3,48},{4,64},{5,80},{6,96},{7,112},{8,1},{9,1... | collective-permute-start | bytes 786440 | tf_op jit(solution)/shard_map/ppermute | solution.py:355
  61.4 27.2 %all-to-all-start.2 = ((f32[8,3,8,128]{3,2,1,0:T(8,128)}), f32[8,3,8,128]{3,2,1,0:T(8,128)S(1)}, u32[]{:S(2)}, u32[]{:S(2)}) async-start(f32[8,3,8,128]{3,2,1,0:T(8,128)} %broadcast_in_dim.25), calls=%async_computation.2 | async-start | bytes 196608 | tf_op jit(solution)/shard_map/all_to_all | solution.py:305
  69.4 24.8 %copy-start.4 = (f32[64,1024]{1,0:T(8,128)}, f32[64,1024]{1,0:T(8,128)S(1)}, u32[]{:S(2)}) copy-start(f32[64,1024]{1,0:T(8,128)S(1)} %collective-permute-done.7) | copy-start | bytes 786436
  89.5 13.7 %all-to-all-start.3 = ((f32[16,8,8,128]{3,2,1,0:T(8,128)}), f32[16,8,8,128]{3,2,1,0:T(8,128)S(1)}, u32[]{:S(2)}, u32[]{:S(2)}) async-start(f32[16,8,8,128]{3,2,1,0:T(8,128)} %broadcast_in_dim.27), calls=%async_computation.3 | async-start | bytes 1048576 | tf_op jit(solution)/shard_map/all_to_all | solution.py:305
  94.2 89.2 %all-gather.5.cloned.1.call-start = ((), (), s32[]{:S(2)}) async-start(), calls=%async_computation.6 | async-start | bytes 4456448 | tf_op jit(solution)/shard_map/all_gather | solution.py:361
  103.2 8.5 %collective-permute-start.8 = (f32[16,8,8,128]{3,2,1,0:T(8,128)S(1)}, f32[16,8,8,128]{3,2,1,0:T(8,128)S(1)}, u32[]{:S(2)}, u32[]{:S(2)}) collective-permute-start(f32[16,8,8,128]{3,2,1,0:T(8,128)S(1)} %all-to-all-done.3.own_ref), channel_id=1, source_target_pairs={{0,8},{8,0},{16,24},{24,16},{32,40},{40,32},{48,56},{56,48},{64,72... | collective-permute-start | bytes 1572872 | tf_op jit(solution)/shard_map/ppermute | solution.py:362
  104.4 27.7 %copy-start = (s32[3]{0:T(128)}, s32[3]{0:T(128)S(1)}, u32[]{:S(2)}) copy-start(s32[3]{0:T(128)S(1)} %pad_add_fusion.core_ref.at_ref) | copy-start | bytes 40
  105.8 34.6 %all-to-all-start.4 = ((f32[16,24,8,128]{3,2,1,0:T(8,128)}), f32[16,24,8,128]{3,2,1,0:T(8,128)S(1)}, u32[]{:S(2)}, u32[]{:S(2)}) async-start(f32[16,24,8,128]{3,2,1,0:T(8,128)} %broadcast_in_dim.28), calls=%async_computation.4 | async-start | bytes 3145728 | tf_op jit(solution)/shard_map/all_to_all | solution.py:305
  132.1 1.0 copy-start.1
  140.4 3.9 %copy-start.3 = (f32[16,24,8,128]{3,2,1,0:T(8,128)}, f32[16,24,8,128]{3,2,1,0:T(8,128)S(1)}, u32[]{:S(2)}) copy-start(f32[16,24,8,128]{3,2,1,0:T(8,128)S(1)} %all-to-all-done.4.own_ref) | copy-start | bytes 4718596
  140.4 3.9 %collective-permute-start.9 = (f32[16,24,8,128]{3,2,1,0:T(8,128)S(1)}, f32[16,24,8,128]{3,2,1,0:T(8,128)S(1)}, u32[]{:S(2)}, u32[]{:S(2)}) collective-permute-start(f32[16,24,8,128]{3,2,1,0:T(8,128)S(1)} %all-to-all-done.4.own_ref), channel_id=1, source_target_pairs={{0,8},{8,0},{16,24},{24,16},{32,40},{40,32},{48,56},{56,48},{64,72... | collective-permute-start | bytes 4718600 | tf_op jit(solution)/shard_map/ppermute | solution.py:372
  144.3 1.2 copy-start.5
  183.4 9.1 %collective-permute-start.10 = (f32[1024,1024]{1,0:T(8,128)}, f32[1024,1024]{1,0:T(8,128)}, u32[]{:S(2)}, u32[]{:S(2)}) collective-permute-start(f32[1024,1024]{1,0:T(8,128)} %all-gather.5.cloned.1.call-done.match_ref), channel_id=1, source_target_pairs={{0,8},{8,0},{16,24},{24,16},{32,40},{40,32},{48,56},{56,48},{64,72... | collective-permute-start | bytes 12582920 | tf_op jit(solution)/shard_map/ppermute | solution.py:378
Sparse Core Ops, SparseCore 0:
  41.5 59.6 all-gather.2
  103.6 65.3 all-gather.4
where the time goes:
time: 208 us; the launch traced here: 207 us
  Pallas kernels  74.9 us (36%)
  starting transfers between devices  63.9 us (31%)
  waiting for transfers between devices  44.1 us (21%)
  between operations  14.3 us (7%)
  local copies, waits for them, and re-layouts  7.36 us (4%)
  other arithmetic  2.57 us (1%)
    pallas_call x1, Pallas kernels, factor_second(): pl.pallas_call(second_kernel, out_shape=(jax.ShapeDtypeStruct((nb, nb), j...  37.9 us
    all_to_all x3, waiting for transfers between devices, spread(): lax.all_to_all(jnp.broadcast_to(x[None], (size,) + x.shape), axis, 0, 0,...  34.8 us
    pallas_call x1, Pallas kernels, factor_first(): pl.pallas_call(first_kernel, out_shape=jax.ShapeDtypeStruct((nb, nb), jnp...  20.4 us
    all_to_all x3, starting transfers between devices, spread(): lax.all_to_all(jnp.broadcast_to(x[None], (size,) + x.shape), axis, 0, 0,...  18.5 us
    ppermute x7, starting transfers between devices, body(): come = lax.ppermute(piece, 'col', [(0, s), (1, (s + 1) % ncol)])  17.1 us
    pallas_call x2, Pallas kernels, update(): pl.pallas_call(functools.partial(update_kernel, flip), grid_spec=pltpu.Pr...  16.5 us
    ppermute x1, starting transfers between devices, body(): match = lax.ppermute(rows_slab, ('row', 'col'), pairs)  9.83 us
    all_to_all x1, starting transfers between devices, body(): heads = lax.all_to_all(heads, 'row', 0, 0, tiled=True)  8.15 us
  transfers between devices with their start and end apart: 18, of which 7 were waited for; matrix products, arithmetic and copies ran while one was open for 3% of the time, Pallas kernels for 32%

commit v1 on v0

--- a/solution.py
+++ b/solution.py
@@ -25,28 +25,42 @@
     lane = lax.broadcasted_iota(jnp.int32, shape, 1)
     sub = lax.broadcasted_iota(jnp.int32, shape, 0)
     count = len(rows)
+    diag = [lane_of(rows[0], k) for k in range(SUB)]
     for p in range(count):
         at = SUB * p
         panel = (lane >= at) & (lane < at + SUB)
-        row = rows[p]
-        diag = [lane_of(row, at + k) for k in range(SUB)]
-        row = jnp.where(panel, jnp.where(lane == sub + at, 1.0, 0.0), row)
+        more = p + 1 < count
+        if more:
+            ahead = [lane_of(rows[p + 1], at + SUB + k) for k in range(SUB)]
+            near = [lane_of(rows[p + 1], at + k) for k in range(SUB)]
+            below = jnp.where(panel, 0.0, rows[p + 1])
+        row = jnp.where(panel, jnp.where(lane == sub + at, 1.0, 0.0), rows[p])
         inv, tops, low = [], [], {}
         for k in range(SUB):
             scale = lax.rsqrt(sub_of(diag[k], k))
             inv.append(scale)
             mult = diag[k] * scale
-            top = sub_of(row, k) * scale
-            tops.append(top)
             for j in range(k + 1, SUB):
                 low[j, k] = sub_of(diag[j], k) * scale
                 diag[j] = diag[j] - mult * low[j, k]
+            top = sub_of(row, k) * scale
+            tops.append(top)
             row = row - mult * top
+            if more:
+                side = near[k] * scale
+                for j in range(k + 1, SUB):
+                    near[j] = near[j] - side * low[j, k]
+                for j in range(SUB):
+                    ahead[j] = ahead[j] - side * sub_of(side, j)
+                below = below - side * top
         done = tops[0]
         for k in range(1, SUB):
             done = jnp.where(sub == k, tops[k], done)
         rows[p] = jnp.where(lane <= sub + at, done, 0.0)
-        for i in range(p + 1, count):
+        if more:
+            rows[p + 1] = below
+            diag = ahead
+        for i in range(p + 2, count):
             cols = [lane_of(rows[i], at + k) for k in range(SUB)]
             rest = jnp.where(panel, 0.0, rows[i])
             for k in range(SUB):
@@ -229,7 +243,7 @@
         in_specs=[SMEM] + [VMEM] * 5,
         out_specs=(VMEM,) * 5,
         scratch_shapes=[pltpu.VMEM((nb, nb), jnp.float32)] * 2 + [pltpu.VMEM((order, qn), jnp.float32)],
-        compiler_params=pltpu.CompilerParams(vmem_limit_bytes=60 * 2**20),
+        compiler_params=pltpu.CompilerParams(vmem_limit_bytes=32 * 2**20),
         cost_estimate=pl.CostEstimate(flops=300 * nb**3, bytes_accessed=40 * nb * nb, transcendentals=0),
         name="factor_second",
     )(at, own, other, first, mine, desc)
@@ -291,7 +305,7 @@
         ),
         out_shape=jax.ShapeDtypeStruct((nb, stored), jnp.float32),
         input_output_aliases={6: 0} if flip else {},
-        compiler_params=pltpu.CompilerParams(vmem_limit_bytes=60 * 2**20),
+        compiler_params=pltpu.CompilerParams(vmem_limit_bytes=20 * 2**20),
         cost_estimate=pl.CostEstimate(
             flops=6 * nb * stored * order // 2, bytes_accessed=4 * nb * stored + 2 * stored * order,
             transcendentals=0,

time: 208 us -> 204 us (0.981)
  Pallas kernels: 74.9 us -> 57.3 us
  local copies, waits for them, and re-layouts: 7.36 us -> 17.3 us
  waiting for transfers between devices: 44.1 us -> 47.4 us
    unnamed x13 -> x21, local copies, waits for them, and re-layouts: 2.87 us -> 12.8 us
    pallas_call x1, Pallas kernels: 37.9 us -> 31.1 us  [factor_second(): pl.pallas_call(second_kernel, out_shape=(jax.ShapeDtypeStruct((nb, nb), j...]
    pallas_call x2, Pallas kernels: 16.5 us -> 10.3 us  [update(): pl.pallas_call(functools.partial(update_kernel, flip), grid_spec=pltpu.Pr...]
    all_to_all x3, waiting for transfers between devices: 34.8 us -> 39.3 us  [spread(): lax.all_to_all(jnp.broadcast_to(x[None], (size,) + x.shape), axis, 0, 0,...]
    pallas_call x1, Pallas kernels: 20.4 us -> 15.9 us  [factor_first(): pl.pallas_call(first_kernel, out_shape=jax.ShapeDtypeStruct((nb, nb), jnp...]
  transfers between devices with their start and end apart: 18 -> 18, of which waited for: 7 -> 7; matrix products, arithmetic and copies ran while one was open for 3% -> 3% of each run, Pallas kernels for 32% -> 26%
where the time goes in v1:
time: 204 us; the launch traced here: 203 us
  starting transfers between devices  63.9 us (31%)
  Pallas kernels  57.3 us (28%)
  waiting for transfers between devices  47.4 us (23%)
  local copies, waits for them, and re-layouts  17.3 us (8%)
  between operations  14.3 us (7%)
  other arithmetic  2.58 us (1%)
    all_to_all x3, waiting for transfers between devices, spread(): lax.all_to_all(jnp.broadcast_to(x[None], (size,) + x.shape), axis, 0, 0,...  39.3 us
    pallas_call x1, Pallas kernels, factor_second(): pl.pallas_call(second_kernel, out_shape=(jax.ShapeDtypeStruct((nb, nb), j...  31.1 us
    all_to_all x3, starting transfers between devices, spread(): lax.all_to_all(jnp.broadcast_to(x[None], (size,) + x.shape), axis, 0, 0,...  18.5 us
    ppermute x7, starting transfers between devices, body(): come = lax.ppermute(piece, 'col', [(0, s), (1, (s + 1) % ncol)])  17.1 us
    pallas_call x1, Pallas kernels, factor_first(): pl.pallas_call(first_kernel, out_shape=jax.ShapeDtypeStruct((nb, nb), jnp...  15.9 us
    unnamed x21, local copies, waits for them, and re-layouts  12.8 us
    pallas_call x2, Pallas kernels, update(): pl.pallas_call(functools.partial(update_kernel, flip), grid_spec=pltpu.Pr...  10.3 us
    ppermute x1, starting transfers between devices, body(): match = lax.ppermute(rows_slab, ('row', 'col'), pairs)  9.83 us
  transfers between devices with their start and end apart: 18, of which 7 were waited for; matrix products, arithmetic and copies ran while one was open for 3% of the time, Pallas kernels for 26%

profile of v1, /device:TPU:9, one launch (start us, length us, event | category | flops | bytes accessed | tf_op | source)
XLA Modules:
  0.0 202.8 jit_solution(16369702062616880936)
XLA Ops:
  7.2 1.4 slice_select_fusion
  8.6 7.5 %collective-permute-start = (f32[64,512]{1,0:T(8,128)S(1)}, f32[64,512]{1,0:T(8,128)S(1)}, u32[]{:S(2)}, u32[]{:S(2)}) collective-permute-start(f32[64,512]{1,0:T(8,128)S(1)} %get-tuple-element.43), channel_id=1, source_target_pairs={{0,7},{1,0},{8,15},{9,8},{16,23},{17,16},{24,31},{25,24},{32,39},{... | collective-permute-start | bytes 393224 | tf_op jit(solution)/shard_map/ppermute | solution.py:350
  16.1 1.3 collective-permute-start.1
  17.4 8.1 %all-to-all-start = ((f32[32,4,8,128]{3,2,1,0:T(8,128)}), f32[32,4,8,128]{3,2,1,0:T(8,128)S(1)}, u32[]{:S(2)}, u32[]{:S(2)}) async-start(f32[32,4,8,128]{3,2,1,0:T(8,128)} %bitcast.24), calls=%async_computation | async-start | bytes 1048576 | tf_op jit(solution)/shard_map/all_to_all | solution.py:343
  25.5 0.0 all-gather.3.cloned.1.call-start
  25.6 1.3 collective-permute-start.2
  26.9 1.3 collective-permute-start.3
  28.2 1.3 collective-permute-start.4
  29.5 0.0 collective-permute-done
  29.5 1.3 collective-permute-start.5
  30.8 0.0 collective-permute-done.1
  30.8 3.1 %collective-permute-start.6 = (f32[64,512]{1,0:T(8,128)S(1)}, f32[64,512]{1,0:T(8,128)S(1)}, u32[]{:S(2)}, u32[]{:S(2)}) collective-permute-start(f32[64,512]{1,0:T(8,128)S(1)} %get-tuple-element.37), channel_id=1, source_target_pairs={{0,1},{1,2},{8,9},{9,10},{16,17},{17,18},{24,25},{25,26},{32,33},{... | collective-permute-start | bytes 393224 | tf_op jit(solution)/shard_map/ppermute | solution.py:350
  33.9 1.2 collective-permute-done.2
  35.2 0.0 collective-permute-done.3
  35.2 0.0 collective-permute-done.4
  35.2 1.5 collective-permute-done.5
  36.7 2.8 %collective-permute-done.6 = f32[64,512]{1,0:T(8,128)S(1)} collective-permute-done((f32[64,512]{1,0:T(8,128)S(1)}, f32[64,512]{1,0:T(8,128)S(1)}, u32[]{:S(2)}, u32[]{:S(2)}) %collective-permute-start.6) | collective-permute-done | bytes 131104 | tf_op jit(solution)/shard_map/ppermute | solution.py:350
  39.5 1.1 select_select_fusion
  40.6 0.0 all-to-all-done
  40.6 0.0 copy-start.8
  40.6 0.7 copy-done.8
  41.3 0.0 all-gather.3.cloned.1.call-update
  41.4 1.7 copy.9
  43.0 7.9 %all-to-all-start.1 = ((f32[32,2,8,128]{3,2,1,0:T(8,128)}), f32[32,2,8,128]{3,2,1,0:T(8,128)S(1)}, u32[]{:S(2)}, u32[]{:S(2)}) async-start(f32[32,2,8,128]{3,2,1,0:T(8,128)} %bitcast.8), calls=%async_computation.1 | async-start | bytes 524288 | tf_op jit(solution)/shard_map/all_to_all | solution.py:360
  50.9 9.8 %collective-permute-start.7 = (f32[64,1024]{1,0:T(8,128)}, f32[64,1024]{1,0:T(8,128)S(1)}, u32[]{:S(2)}, u32[]{:S(2)}) collective-permute-start(f32[64,1024]{1,0:T(8,128)} %copy-done.8), channel_id=1, source_target_pairs={{0,0},{1,16},{2,32},{3,48},{4,64},{5,80},{6,96},{7,112},{8,1},{9,1... | collective-permute-start | bytes 786440 | tf_op jit(solution)/shard_map/ppermute | solution.py:369
  60.8 0.0 all-to-all-done.1
  60.8 0.6 broadcast_in_dim.25
  61.5 7.9 %all-to-all-start.2 = ((f32[8,3,8,128]{3,2,1,0:T(8,128)}), f32[8,3,8,128]{3,2,1,0:T(8,128)S(1)}, u32[]{:S(2)}, u32[]{:S(2)}) async-start(f32[8,3,8,128]{3,2,1,0:T(8,128)} %broadcast_in_dim.25), calls=%async_computation.2 | async-start | bytes 196608 | tf_op jit(solution)/shard_map/all_to_all | solution.py:319
  69.4 0.0 collective-permute-done.7
  69.4 0.0 copy-start.9
  69.4 19.3 %all-to-all-done.2 = f32[8,3,8,128]{3,2,1,0:T(8,128)S(1)} async-done(((f32[8,3,8,128]{3,2,1,0:T(8,128)}), f32[8,3,8,128]{3,2,1,0:T(8,128)S(1)}, u32[]{:S(2)}, u32[]{:S(2)}) %all-to-all-start.2) | async-done | bytes 98336 | tf_op jit(solution)/shard_map/all_to_all | solution.py:319
  88.7 0.8 broadcast_in_dim.27
  89.5 4.7 %all-to-all-start.3 = ((f32[16,8,8,128]{3,2,1,0:T(8,128)}), f32[16,8,8,128]{3,2,1,0:T(8,128)S(1)}, u32[]{:S(2)}, u32[]{:S(2)}) async-start(f32[16,8,8,128]{3,2,1,0:T(8,128)} %broadcast_in_dim.27), calls=%async_computation.3 | async-start | bytes 1048576 | tf_op jit(solution)/shard_map/all_to_all | solution.py:319
  94.2 0.0 all-gather.5.cloned.1.call-start
  94.2 0.0 copy-done.9
  94.2 0.7 all-gather.5.cloned.1.call-update
  94.9 8.3 %all-to-all-done.3.own_ref = f32[16,8,8,128]{3,2,1,0:T(8,128)S(1)} async-done(((f32[16,8,8,128]{3,2,1,0:T(8,128)}), f32[16,8,8,128]{3,2,1,0:T(8,128)S(1)}, u32[]{:S(2)}, u32[]{:S(2)}) %all-to-all-start.3) | async-done | bytes 524320 | tf_op jit(solution)/shard_map/all_to_all | solution.py:319
  103.2 1.2 collective-permute-start.8
  104.4 0.1 pad_add_fusion.core_ref.at_ref
  104.5 1.3 broadcast_in_dim.28
  105.8 5.9 %all-to-all-start.4 = ((f32[16,24,8,128]{3,2,1,0:T(8,128)}), f32[16,24,8,128]{3,2,1,0:T(8,128)S(1)}, u32[]{:S(2)}, u32[]{:S(2)}) async-start(f32[16,24,8,128]{3,2,1,0:T(8,128)} %broadcast_in_dim.28), calls=%async_computation.4 | async-start | bytes 3145728 | tf_op jit(solution)/shard_map/all_to_all | solution.py:319
  111.7 0.0 all-gather.3.cloned.1.call-done.mine_ref
  111.7 0.0 collective-permute-done.8.other_ref
  111.7 15.9 %factor_first.1.first_ref = f32[512,512]{1,0:T(8,128)S(1)} custom-call(s32[3]{0:T(128)S(1)} %pad_add_fusion.core_ref.at_ref, f32[16,8,8,128]{3,2,1,0:T(8,128)S(1)} %all-to-all-done.3.own_ref, f32[16,8,8,128]{3,2,1,0:T(8,128)S(1)} %collective-permute-done.8.other_ref), custom_call_target="tpu_custom_call" | custom-call | flops 20132659200 | bytes 2097152 | tf_op jit(solution)/shard_map/factor_first/pallas_call | solution.py:220
  127.6 0.0 copy-start.6
  127.6 1.0 copy-done.6
  128.6 11.8 %all-to-all-done.4.own_ref = f32[16,24,8,128]{3,2,1,0:T(8,128)S(1)} async-done(((f32[16,24,8,128]{3,2,1,0:T(8,128)}), f32[16,24,8,128]{3,2,1,0:T(8,128)S(1)}, u32[]{:S(2)}, u32[]{:S(2)}) %all-to-all-start.4) | async-done | bytes 1572896 | tf_op jit(solution)/shard_map/all_to_all | solution.py:319
  140.4 0.8 collective-permute-start.9
  141.2 0.0 copy-start.2
  141.2 1.1 copy-done.2
  142.4 1.9 collective-permute-done.9.other_ref
  144.3 0.0 copy-start.3
  144.3 1.4 copy-done.3
  145.7 0.0 copy-start.4
  145.7 1.0 copy-done.4
  146.7 1.6 copy-done.5
  148.3 1.5 copy-done.7
  149.8 31.1 %factor_second.1 = (f32[512,512]{1,0:T(8,128)S(1)}, bf16[512,1024]{1,0:T(8,128)(2,1)S(1)}, bf16[512,1024]{1,0:T(8,128)(2,1)S(1)}, f32[512,256]{1,0:T(8,128)}, f32[1,256]{1,0:T(1,128)}) custom-call(s32[3]{0:T(128)S(1)} %pad_add_fusion.core_ref.at_ref, f32[16,24,8,128]{3,2,1,0:T(8,128)S(1)} %copy-done.3, ...), custom_call_target="tpu_custom_call" | custom-call | flops 40265318400 | bytes 10485760 | tf_op jit(solution)/shard_map/factor_second/pallas_call | solution.py:234
  180.9 0.4 collective-permute-start.10
  181.3 2.2 %copy-done = f32[512,2048]{1,0:T(8,128)S(1)} copy-done((f32[512,2048]{1,0:T(8,128)S(1)}, f32[512,2048]{1,0:T(8,128)}, u32[]{:S(2)}) %copy-start) | copy-done | bytes 4194328
  183.5 2.2 %copy-done.1 = f32[1024,1024]{1,0:T(8,128)S(1)} copy-done((f32[1024,1024]{1,0:T(8,128)S(1)}, f32[1024,1024]{1,0:T(8,128)}, u32[]{:S(2)}) %copy-start.1) | copy-done | bytes 4194328
  185.7 5.8 %update_own.1.refs_0_ = f32[512,2048]{1,0:T(8,128)} custom-call(s32[3]{0:T(128)S(1)} %pad_add_fusion.core_ref.at_ref, f32[512,2048]{1,0:T(8,128)S(1)} %copy-done, f32[1024,1024]{1,0:T(8,128)S(1)} %copy-done.1, bf16[512,1024]{1,0:T(8,128)(2,1)S(1)} %get-tuple-element.30.high_ref, bf16[512,1024]{1,0:T(8,128)(2,1)S(1)} %get-tuple-element.31.low_ref, ...), custom_call_target="tpu_custom_call" | custom-call | flops 3221225472 | bytes 8388608 | tf_op jit(solution)/shard_map/update_own/pallas_call | solution.py:298
  191.5 0.0 collective-permute-done.10.match_ref
  191.5 4.5 %update_other.1 = f32[512,2048]{1,0:T(8,128)} custom-call(s32[3]{0:T(128)S(1)} %pad_add_fusion.core_ref.at_ref, f32[512,2048]{1,0:T(8,128)S(1)} %copy-done, f32[1024,1024]{1,0:T(8,128)S(1)} %collective-permute-done.10.match_ref, bf16[512,1024]{1,0:T(8,128)(2,1)S(1)} %get-tuple-element.30.high_ref, ...), custom_call_target="tpu_custom_call", output_to_operand_aliasing={{}: (6, {})} | custom-call | flops 3221225472 | bytes 8388608 | tf_op jit(solution)/shard_map/update_other/pallas_call | solution.py:298
  (14 shorter events, 0.1 us)
Async XLA Ops:
  8.6 20.9 %collective-permute-start = (f32[64,512]{1,0:T(8,128)S(1)}, f32[64,512]{1,0:T(8,128)S(1)}, u32[]{:S(2)}, u32[]{:S(2)}) collective-permute-start(f32[64,512]{1,0:T(8,128)S(1)} %get-tuple-element.43), channel_id=1, source_target_pairs={{0,7},{1,0},{8,15},{9,8},{16,23},{17,16},{24,31},{25,24},{32,39},{... | collective-permute-start | bytes 393224 | tf_op jit(solution)/shard_map/ppermute | solution.py:350
  16.1 14.7 %collective-permute-start.1 = (f32[64,512]{1,0:T(8,128)S(1)}, f32[64,512]{1,0:T(8,128)S(1)}, u32[]{:S(2)}, u32[]{:S(2)}) collective-permute-start(f32[64,512]{1,0:T(8,128)S(1)} %get-tuple-element.42), channel_id=1, source_target_pairs={{0,6},{1,7},{8,14},{9,15},{16,22},{17,23},{24,30},{25,31},{32,38},... | collective-permute-start | bytes 393224 | tf_op jit(solution)/shard_map/ppermute | solution.py:350
  17.4 23.2 %all-to-all-start = ((f32[32,4,8,128]{3,2,1,0:T(8,128)}), f32[32,4,8,128]{3,2,1,0:T(8,128)S(1)}, u32[]{:S(2)}, u32[]{:S(2)}) async-start(f32[32,4,8,128]{3,2,1,0:T(8,128)} %bitcast.24), calls=%async_computation | async-start | bytes 1048576 | tf_op jit(solution)/shard_map/all_to_all | solution.py:343
  25.5 86.2 %all-gather.3.cloned.1.call-start = ((), (), s32[]{:S(2)}) async-start(), calls=%async_computation.5 | async-start | bytes 2359296 | tf_op jit(solution)/shard_map/all_gather | solution.py:356
  25.6 9.6 %collective-permute-start.2 = (f32[64,512]{1,0:T(8,128)S(1)}, f32[64,512]{1,0:T(8,128)S(1)}, u32[]{:S(2)}, u32[]{:S(2)}) collective-permute-start(f32[64,512]{1,0:T(8,128)S(1)} %get-tuple-element.41), channel_id=1, source_target_pairs={{0,5},{1,6},{8,13},{9,14},{16,21},{17,22},{24,29},{25,30},{32,37},... | collective-permute-start | bytes 393224 | tf_op jit(solution)/shard_map/ppermute | solution.py:350
  26.9 8.3 %collective-permute-start.3 = (f32[64,512]{1,0:T(8,128)S(1)}, f32[64,512]{1,0:T(8,128)S(1)}, u32[]{:S(2)}, u32[]{:S(2)}) collective-permute-start(f32[64,512]{1,0:T(8,128)S(1)} %get-tuple-element.40), channel_id=1, source_target_pairs={{0,4},{1,5},{8,12},{9,13},{16,20},{17,21},{24,28},{25,29},{32,36},... | collective-permute-start | bytes 393224 | tf_op jit(solution)/shard_map/ppermute | solution.py:350
  28.2 7.0 %collective-permute-start.4 = (f32[64,512]{1,0:T(8,128)S(1)}, f32[64,512]{1,0:T(8,128)S(1)}, u32[]{:S(2)}, u32[]{:S(2)}) collective-permute-start(f32[64,512]{1,0:T(8,128)S(1)} %get-tuple-element.39), channel_id=1, source_target_pairs={{0,3},{1,4},{8,11},{9,12},{16,19},{17,20},{24,27},{25,28},{32,35},... | collective-permute-start | bytes 393224 | tf_op jit(solution)/shard_map/ppermute | solution.py:350
  29.5 7.2 %collective-permute-start.5 = (f32[64,512]{1,0:T(8,128)S(1)}, f32[64,512]{1,0:T(8,128)S(1)}, u32[]{:S(2)}, u32[]{:S(2)}) collective-permute-start(f32[64,512]{1,0:T(8,128)S(1)} %get-tuple-element.38), channel_id=1, source_target_pairs={{0,2},{1,3},{8,10},{9,11},{16,18},{17,19},{24,26},{25,27},{32,34},... | collective-permute-start | bytes 393224 | tf_op jit(solution)/shard_map/ppermute | solution.py:350
  30.8 8.7 %collective-permute-start.6 = (f32[64,512]{1,0:T(8,128)S(1)}, f32[64,512]{1,0:T(8,128)S(1)}, u32[]{:S(2)}, u32[]{:S(2)}) collective-permute-start(f32[64,512]{1,0:T(8,128)S(1)} %get-tuple-element.37), channel_id=1, source_target_pairs={{0,1},{1,2},{8,9},{9,10},{16,17},{17,18},{24,25},{25,26},{32,33},{... | collective-permute-start | bytes 393224 | tf_op jit(solution)/shard_map/ppermute | solution.py:350
  40.6 0.7 copy-start.8
  43.0 17.7 %all-to-all-start.1 = ((f32[32,2,8,128]{3,2,1,0:T(8,128)}), f32[32,2,8,128]{3,2,1,0:T(8,128)S(1)}, u32[]{:S(2)}, u32[]{:S(2)}) async-start(f32[32,2,8,128]{3,2,1,0:T(8,128)} %bitcast.8), calls=%async_computation.1 | async-start | bytes 524288 | tf_op jit(solution)/shard_map/all_to_all | solution.py:360
  50.9 18.5 %collective-permute-start.7 = (f32[64,1024]{1,0:T(8,128)}, f32[64,1024]{1,0:T(8,128)S(1)}, u32[]{:S(2)}, u32[]{:S(2)}) collective-permute-start(f32[64,1024]{1,0:T(8,128)} %copy-done.8), channel_id=1, source_target_pairs={{0,0},{1,16},{2,32},{3,48},{4,64},{5,80},{6,96},{7,112},{8,1},{9,1... | collective-permute-start | bytes 786440 | tf_op jit(solution)/shard_map/ppermute | solution.py:369
  61.5 27.2 %all-to-all-start.2 = ((f32[8,3,8,128]{3,2,1,0:T(8,128)}), f32[8,3,8,128]{3,2,1,0:T(8,128)S(1)}, u32[]{:S(2)}, u32[]{:S(2)}) async-start(f32[8,3,8,128]{3,2,1,0:T(8,128)} %broadcast_in_dim.25), calls=%async_computation.2 | async-start | bytes 196608 | tf_op jit(solution)/shard_map/all_to_all | solution.py:319
  69.4 24.8 %copy-start.9 = (f32[64,1024]{1,0:T(8,128)}, f32[64,1024]{1,0:T(8,128)S(1)}, u32[]{:S(2)}) copy-start(f32[64,1024]{1,0:T(8,128)S(1)} %collective-permute-done.7) | copy-start | bytes 786436
  89.5 13.7 %all-to-all-start.3 = ((f32[16,8,8,128]{3,2,1,0:T(8,128)}), f32[16,8,8,128]{3,2,1,0:T(8,128)S(1)}, u32[]{:S(2)}, u32[]{:S(2)}) async-start(f32[16,8,8,128]{3,2,1,0:T(8,128)} %broadcast_in_dim.27), calls=%async_computation.3 | async-start | bytes 1048576 | tf_op jit(solution)/shard_map/all_to_all | solution.py:319
  94.2 86.8 %all-gather.5.cloned.1.call-start = ((), (), s32[]{:S(2)}) async-start(), calls=%async_computation.6 | async-start | bytes 4456448 | tf_op jit(solution)/shard_map/all_gather | solution.py:375
  103.2 8.5 %collective-permute-start.8 = (f32[16,8,8,128]{3,2,1,0:T(8,128)S(1)}, f32[16,8,8,128]{3,2,1,0:T(8,128)S(1)}, u32[]{:S(2)}, u32[]{:S(2)}) collective-permute-start(f32[16,8,8,128]{3,2,1,0:T(8,128)S(1)} %all-to-all-done.3.own_ref), channel_id=1, source_target_pairs={{0,8},{8,0},{16,24},{24,16},{32,40},{40,32},{48,56},{56,48},{64,72... | collective-permute-start | bytes 1572872 | tf_op jit(solution)/shard_map/ppermute | solution.py:376
  105.8 34.6 %all-to-all-start.4 = ((f32[16,24,8,128]{3,2,1,0:T(8,128)}), f32[16,24,8,128]{3,2,1,0:T(8,128)S(1)}, u32[]{:S(2)}, u32[]{:S(2)}) async-start(f32[16,24,8,128]{3,2,1,0:T(8,128)} %broadcast_in_dim.28), calls=%async_computation.4 | async-start | bytes 3145728 | tf_op jit(solution)/shard_map/all_to_all | solution.py:319
  127.6 1.0 copy-start.6
  140.4 3.9 %collective-permute-start.9 = (f32[16,24,8,128]{3,2,1,0:T(8,128)S(1)}, f32[16,24,8,128]{3,2,1,0:T(8,128)S(1)}, u32[]{:S(2)}, u32[]{:S(2)}) collective-permute-start(f32[16,24,8,128]{3,2,1,0:T(8,128)S(1)} %all-to-all-done.4.own_ref), channel_id=1, source_target_pairs={{0,8},{8,0},{16,24},{24,16},{32,40},{40,32},{48,56},{56,48},{64,72... | collective-permute-start | bytes 4718600 | tf_op jit(solution)/shard_map/ppermute | solution.py:386
  141.2 1.1 copy-start.2
  144.3 1.4 copy-start.3
  145.7 1.0 copy-start.4
  146.7 1.6 copy-start.5
  148.3 1.5 copy-start.7
  180.9 10.5 %collective-permute-start.10 = (f32[1024,1024]{1,0:T(8,128)}, f32[1024,1024]{1,0:T(8,128)S(1)}, u32[]{:S(2)}, u32[]{:S(2)}) collective-permute-start(f32[1024,1024]{1,0:T(8,128)} %all-gather.5.cloned.1.call-done.match_ref), channel_id=1, source_target_pairs={{0,8},{8,0},{16,24},{24,16},{32,40},{40,32},{48,56},{56,48},{64,72... | collective-permute-start | bytes 12582920 | tf_op jit(solution)/shard_map/ppermute | solution.py:392
  181.3 2.2 %copy-start = (f32[512,2048]{1,0:T(8,128)S(1)}, f32[512,2048]{1,0:T(8,128)}, u32[]{:S(2)}) copy-start(f32[512,2048]{1,0:T(8,128)} %gram_ref.3) | copy-start | bytes 12582916
  183.5 2.2 %copy-start.1 = (f32[1024,1024]{1,0:T(8,128)S(1)}, f32[1024,1024]{1,0:T(8,128)}, u32[]{:S(2)}) copy-start(f32[1024,1024]{1,0:T(8,128)} %all-gather.5.cloned.1.call-done.match_ref) | copy-start | bytes 12582916
Sparse Core Ops, SparseCore 0:
  41.5 59.6 all-gather.2
  103.6 65.3 all-gather.4

commit v2 on v1

--- a/solution.py
+++ b/solution.py
@@ -340,16 +340,17 @@
     chunk = nb // nrow
     heads = desc.reshape(nrow, chunk // SUB, SUB, qn // TILE, TILE).transpose(0, 1, 3, 2, 4)
     heads = heads.reshape(nrow, -1, SUB, TILE)
-    heads = lax.all_to_all(heads, "row", 0, 0, tiled=True)
-
     front = front.reshape(ncol, slab, nb)
     slab0 = jnp.where(pcol == 0, front[0], 0.0)
     slab1 = jnp.where(pcol == 1, front[1], 0.0)
     for s in range(1, ncol):
         piece = jnp.where(pcol == 0, front[s], front[(s + 1) % ncol])
         come = lax.ppermute(piece, "col", [(0, s), (1, (s + 1) % ncol)])
+        if s == 1:
+            come, heads = lax.optimization_barrier((come, heads))
         slab0 = jnp.where(pcol == s, come, slab0)
         slab1 = jnp.where(pcol == (s + 1) % ncol, come, slab1)
+    heads = lax.all_to_all(heads, "row", 0, 0, tiled=True)
     heads, slab0, slab1 = lax.optimization_barrier((heads, slab0, slab1))
     rows_slab = jnp.concatenate([slab0, slab1], axis=1)
 

time: 204 us -> 202 us (level)
  starting transfers between devices: 63.9 us -> 58.4 us
  waiting for transfers between devices: 47.4 us -> 51.2 us
    ppermute x7, waiting for transfers between devices: 5.54 us -> 8.82 us  [body(): come = lax.ppermute(piece, 'col', [(0, s), (1, (s + 1) % ncol)])]
    ppermute x1, starting transfers between devices: 9.83 us -> 6.85 us  [body(): match = lax.ppermute(rows_slab, ('row', 'col'), pairs)]
    ppermute x7, starting transfers between devices: 17.1 us -> 14.6 us  [body(): come = lax.ppermute(piece, 'col', [(0, s), (1, (s + 1) % ncol)])]
  transfers between devices with their start and end apart: 18 -> 18, of which waited for: 7 -> 8; matrix products, arithmetic and copies ran while one was open for 3% -> 3% of each run, Pallas kernels for 26% -> 26%
where the time goes in v2:
time: 202 us; the launch traced here: 201 us
  starting transfers between devices  58.4 us (29%)
  Pallas kernels  57.3 us (28%)
  waiting for transfers between devices  51.2 us (25%)
  local copies, waits for them, and re-layouts  17 us (8%)
  between operations  14.3 us (7%)
  other arithmetic  2.6 us (1%)
    all_to_all x3, waiting for transfers between devices, spread(): lax.all_to_all(jnp.broadcast_to(x[None], (size,) + x.shape), axis, 0, 0,...  37.6 us
    pallas_call x1, Pallas kernels, factor_second(): pl.pallas_call(second_kernel, out_shape=(jax.ShapeDtypeStruct((nb, nb), j...  31.1 us
    all_to_all x3, starting transfers between devices, spread(): lax.all_to_all(jnp.broadcast_to(x[None], (size,) + x.shape), axis, 0, 0,...  16.8 us
    pallas_call x1, Pallas kernels, factor_first(): pl.pallas_call(first_kernel, out_shape=jax.ShapeDtypeStruct((nb, nb), jnp...  15.9 us
    ppermute x7, starting transfers between devices, body(): come = lax.ppermute(piece, 'col', [(0, s), (1, (s + 1) % ncol)])  14.6 us
    unnamed x21, local copies, waits for them, and re-layouts  12.5 us
    pallas_call x2, Pallas kernels, update(): pl.pallas_call(functools.partial(update_kernel, flip), grid_spec=pltpu.Pr...  10.3 us
    ppermute x7, waiting for transfers between devices, body(): come = lax.ppermute(piece, 'col', [(0, s), (1, (s + 1) % ncol)])  8.82 us
  transfers between devices with their start and end apart: 18, of which 8 were waited for; matrix products, arithmetic and copies ran while one was open for 3% of the time, Pallas kernels for 26%

profile of v2, /device:TPU:9, one launch (start us, length us, event | category | flops | bytes accessed | tf_op | source)
XLA Modules:
  0.0 200.8 jit_solution(16871826521709871024)
XLA Ops:
  7.2 1.4 slice_select_fusion
  8.6 3.5 %collective-permute-start = (f32[64,512]{1,0:T(8,128)S(1)}, f32[64,512]{1,0:T(8,128)S(1)}, u32[]{:S(2)}, u32[]{:S(2)}) collective-permute-start(f32[64,512]{1,0:T(8,128)S(1)} %get-tuple-element.47), channel_id=1, source_target_pairs={{0,1},{1,2},{8,9},{9,10},{16,17},{17,18},{24,25},{25,26},{32,33},{... | collective-permute-start | bytes 393224 | tf_op jit(solution)/shard_map/ppermute | solution.py:348
  12.1 4.6 %collective-permute-start.1 = (f32[64,512]{1,0:T(8,128)S(1)}, f32[64,512]{1,0:T(8,128)S(1)}, u32[]{:S(2)}, u32[]{:S(2)}) collective-permute-start(f32[64,512]{1,0:T(8,128)S(1)} %get-tuple-element.46), channel_id=1, source_target_pairs={{0,7},{1,0},{8,15},{9,8},{16,23},{17,16},{24,31},{25,24},{32,39},{... | collective-permute-start | bytes 393224 | tf_op jit(solution)/shard_map/ppermute | solution.py:348
  16.7 0.0 collective-permute-done
  16.8 8.1 %all-to-all-start = ((f32[32,4,8,128]{3,2,1,0:T(8,128)}), f32[32,4,8,128]{3,2,1,0:T(8,128)S(1)}, u32[]{:S(2)}, u32[]{:S(2)}) async-start(f32[32,4,8,128]{3,2,1,0:T(8,128)} %bitcast.24), calls=%async_computation | async-start | bytes 1048576 | tf_op jit(solution)/shard_map/all_to_all | solution.py:353
  24.9 0.0 all-gather.3.cloned.1.call-start
  25.0 1.3 collective-permute-start.2
  26.3 1.3 collective-permute-start.3
  27.6 1.3 collective-permute-start.4
  28.9 1.3 collective-permute-start.5
  30.2 0.0 collective-permute-done.1
  30.2 1.3 collective-permute-start.6
  31.5 6.0 %collective-permute-done.2 = f32[64,512]{1,0:T(8,128)S(1)} collective-permute-done((f32[64,512]{1,0:T(8,128)S(1)}, f32[64,512]{1,0:T(8,128)S(1)}, u32[]{:S(2)}, u32[]{:S(2)}) %collective-permute-start.2) | collective-permute-done | bytes 131104 | tf_op jit(solution)/shard_map/ppermute | solution.py:348
  37.5 2.8 %collective-permute-done.3 = f32[64,512]{1,0:T(8,128)S(1)} collective-permute-done((f32[64,512]{1,0:T(8,128)S(1)}, f32[64,512]{1,0:T(8,128)S(1)}, u32[]{:S(2)}, u32[]{:S(2)}) %collective-permute-start.3) | collective-permute-done | bytes 131104 | tf_op jit(solution)/shard_map/ppermute | solution.py:348
  40.3 0.0 collective-permute-done.4
  40.3 0.0 collective-permute-done.5
  40.3 0.0 collective-permute-done.6
  40.3 1.1 select_select_fusion
  41.4 0.0 all-to-all-done
  41.5 0.0 copy-start.8
  41.5 0.7 copy-done.8
  42.2 0.0 all-gather.3.cloned.1.call-update
  42.2 1.7 copy.9
  43.9 7.9 %all-to-all-start.1 = ((f32[32,2,8,128]{3,2,1,0:T(8,128)}), f32[32,2,8,128]{3,2,1,0:T(8,128)S(1)}, u32[]{:S(2)}, u32[]{:S(2)}) async-start(f32[32,2,8,128]{3,2,1,0:T(8,128)} %bitcast.8), calls=%async_computation.1 | async-start | bytes 524288 | tf_op jit(solution)/shard_map/all_to_all | solution.py:361
  51.8 6.8 %collective-permute-start.7 = (f32[64,1024]{1,0:T(8,128)}, f32[64,1024]{1,0:T(8,128)S(1)}, u32[]{:S(2)}, u32[]{:S(2)}) collective-permute-start(f32[64,1024]{1,0:T(8,128)} %copy-done.8), channel_id=1, source_target_pairs={{0,0},{1,16},{2,32},{3,48},{4,64},{5,80},{6,96},{7,112},{8,1},{9,1... | collective-permute-start | bytes 786440 | tf_op jit(solution)/shard_map/ppermute | solution.py:370
  58.6 1.1 all-to-all-done.1
  59.8 0.7 broadcast_in_dim.25
  60.4 7.8 %all-to-all-start.2 = ((f32[8,3,8,128]{3,2,1,0:T(8,128)}), f32[8,3,8,128]{3,2,1,0:T(8,128)S(1)}, u32[]{:S(2)}, u32[]{:S(2)}) async-start(f32[8,3,8,128]{3,2,1,0:T(8,128)} %broadcast_in_dim.25), calls=%async_computation.2 | async-start | bytes 196608 | tf_op jit(solution)/shard_map/all_to_all | solution.py:319
  68.2 1.0 collective-permute-done.7
  69.2 0.0 copy-start.9
  69.2 19.4 %all-to-all-done.2 = f32[8,3,8,128]{3,2,1,0:T(8,128)S(1)} async-done(((f32[8,3,8,128]{3,2,1,0:T(8,128)}), f32[8,3,8,128]{3,2,1,0:T(8,128)S(1)}, u32[]{:S(2)}, u32[]{:S(2)}) %all-to-all-start.2) | async-done | bytes 98336 | tf_op jit(solution)/shard_map/all_to_all | solution.py:319
  88.6 0.8 broadcast_in_dim.27
  89.4 3.5 %all-to-all-start.3 = ((f32[16,8,8,128]{3,2,1,0:T(8,128)}), f32[16,8,8,128]{3,2,1,0:T(8,128)S(1)}, u32[]{:S(2)}, u32[]{:S(2)}) async-start(f32[16,8,8,128]{3,2,1,0:T(8,128)} %broadcast_in_dim.27), calls=%async_computation.3 | async-start | bytes 1048576 | tf_op jit(solution)/shard_map/all_to_all | solution.py:319
  92.9 0.0 all-gather.5.cloned.1.call-start
  92.9 0.0 copy-done.9
  92.9 0.7 all-gather.5.cloned.1.call-update
  93.6 6.5 %all-to-all-done.3.own_ref = f32[16,8,8,128]{3,2,1,0:T(8,128)S(1)} async-done(((f32[16,8,8,128]{3,2,1,0:T(8,128)}), f32[16,8,8,128]{3,2,1,0:T(8,128)S(1)}, u32[]{:S(2)}, u32[]{:S(2)}) %all-to-all-start.3) | async-done | bytes 524320 | tf_op jit(solution)/shard_map/all_to_all | solution.py:319
  100.1 2.8 %collective-permute-start.8 = (f32[16,8,8,128]{3,2,1,0:T(8,128)S(1)}, f32[16,8,8,128]{3,2,1,0:T(8,128)S(1)}, u32[]{:S(2)}, u32[]{:S(2)}) collective-permute-start(f32[16,8,8,128]{3,2,1,0:T(8,128)S(1)} %all-to-all-done.3.own_ref), channel_id=1, source_target_pairs={{0,8},{8,0},{16,24},{24,16},{32,40},{40,32},{48,56},{56,48},{64,72... | collective-permute-start | bytes 1572872 | tf_op jit(solution)/shard_map/ppermute | solution.py:377
  102.9 0.1 pad_add_fusion.core_ref.at_ref
  103.0 1.3 broadcast_in_dim.28
  104.3 5.6 %all-to-all-start.4 = ((f32[16,24,8,128]{3,2,1,0:T(8,128)}), f32[16,24,8,128]{3,2,1,0:T(8,128)S(1)}, u32[]{:S(2)}, u32[]{:S(2)}) async-start(f32[16,24,8,128]{3,2,1,0:T(8,128)} %broadcast_in_dim.28), calls=%async_computation.4 | async-start | bytes 3145728 | tf_op jit(solution)/shard_map/all_to_all | solution.py:319
  109.9 0.0 all-gather.3.cloned.1.call-done.mine_ref
  110.0 0.0 collective-permute-done.8.other_ref
  110.0 15.9 %factor_first.1.first_ref = f32[512,512]{1,0:T(8,128)S(1)} custom-call(s32[3]{0:T(128)S(1)} %pad_add_fusion.core_ref.at_ref, f32[16,8,8,128]{3,2,1,0:T(8,128)S(1)} %all-to-all-done.3.own_ref, f32[16,8,8,128]{3,2,1,0:T(8,128)S(1)} %collective-permute-done.8.other_ref), custom_call_target="tpu_custom_call" | custom-call | flops 20132659200 | bytes 2097152 | tf_op jit(solution)/shard_map/factor_first/pallas_call | solution.py:220
  125.9 0.0 copy-start.6
  125.9 1.0 copy-done.6
  126.9 11.8 %all-to-all-done.4.own_ref = f32[16,24,8,128]{3,2,1,0:T(8,128)S(1)} async-done(((f32[16,24,8,128]{3,2,1,0:T(8,128)}), f32[16,24,8,128]{3,2,1,0:T(8,128)S(1)}, u32[]{:S(2)}, u32[]{:S(2)}) %all-to-all-start.4) | async-done | bytes 1572896 | tf_op jit(solution)/shard_map/all_to_all | solution.py:319
  138.6 0.8 collective-permute-start.9
  139.5 0.0 copy-start.2
  139.5 1.1 copy-done.2
  140.6 1.9 collective-permute-done.9.other_ref
  142.5 0.0 copy-start.3
  142.5 1.4 copy-done.3
  143.9 0.0 copy-start.4
  143.9 1.0 copy-done.4
  145.0 1.6 copy-done.5
  146.6 1.2 copy-done.7
  147.8 31.1 %factor_second.1 = (f32[512,512]{1,0:T(8,128)S(1)}, bf16[512,1024]{1,0:T(8,128)(2,1)S(1)}, bf16[512,1024]{1,0:T(8,128)(2,1)S(1)}, f32[512,256]{1,0:T(8,128)}, f32[1,256]{1,0:T(1,128)}) custom-call(s32[3]{0:T(128)S(1)} %pad_add_fusion.core_ref.at_ref, f32[16,24,8,128]{3,2,1,0:T(8,128)S(1)} %copy-done.3, ...), custom_call_target="tpu_custom_call" | custom-call | flops 40265318400 | bytes 10485760 | tf_op jit(solution)/shard_map/factor_second/pallas_call | solution.py:234
  178.9 0.4 collective-permute-start.10
  179.3 2.2 %copy-done = f32[512,2048]{1,0:T(8,128)S(1)} copy-done((f32[512,2048]{1,0:T(8,128)S(1)}, f32[512,2048]{1,0:T(8,128)}, u32[]{:S(2)}) %copy-start) | copy-done | bytes 4194328
  181.5 2.2 %copy-done.1 = f32[1024,1024]{1,0:T(8,128)S(1)} copy-done((f32[1024,1024]{1,0:T(8,128)S(1)}, f32[1024,1024]{1,0:T(8,128)}, u32[]{:S(2)}) %copy-start.1) | copy-done | bytes 4194328
  183.6 5.8 %update_own.1.refs_0_ = f32[512,2048]{1,0:T(8,128)} custom-call(s32[3]{0:T(128)S(1)} %pad_add_fusion.core_ref.at_ref, f32[512,2048]{1,0:T(8,128)S(1)} %copy-done, f32[1024,1024]{1,0:T(8,128)S(1)} %copy-done.1, bf16[512,1024]{1,0:T(8,128)(2,1)S(1)} %get-tuple-element.34.high_ref, bf16[512,1024]{1,0:T(8,128)(2,1)S(1)} %get-tuple-element.35.low_ref, ...), custom_call_target="tpu_custom_call" | custom-call | flops 3221225472 | bytes 8388608 | tf_op jit(solution)/shard_map/update_own/pallas_call | solution.py:298
  189.4 0.0 collective-permute-done.10.match_ref
  189.5 4.5 %update_other.1 = f32[512,2048]{1,0:T(8,128)} custom-call(s32[3]{0:T(128)S(1)} %pad_add_fusion.core_ref.at_ref, f32[512,2048]{1,0:T(8,128)S(1)} %copy-done, f32[1024,1024]{1,0:T(8,128)S(1)} %collective-permute-done.10.match_ref, bf16[512,1024]{1,0:T(8,128)(2,1)S(1)} %get-tuple-element.34.high_ref, ...), custom_call_target="tpu_custom_call", output_to_operand_aliasing={{}: (6, {})} | custom-call | flops 3221225472 | bytes 8388608 | tf_op jit(solution)/shard_map/update_other/pallas_call | solution.py:298
  (14 shorter events, 0.1 us)
Async XLA Ops:
  8.6 8.2 %collective-permute-start = (f32[64,512]{1,0:T(8,128)S(1)}, f32[64,512]{1,0:T(8,128)S(1)}, u32[]{:S(2)}, u32[]{:S(2)}) collective-permute-start(f32[64,512]{1,0:T(8,128)S(1)} %get-tuple-element.47), channel_id=1, source_target_pairs={{0,1},{1,2},{8,9},{9,10},{16,17},{17,18},{24,25},{25,26},{32,33},{... | collective-permute-start | bytes 393224 | tf_op jit(solution)/shard_map/ppermute | solution.py:348
  12.1 18.0 %collective-permute-start.1 = (f32[64,512]{1,0:T(8,128)S(1)}, f32[64,512]{1,0:T(8,128)S(1)}, u32[]{:S(2)}, u32[]{:S(2)}) collective-permute-start(f32[64,512]{1,0:T(8,128)S(1)} %get-tuple-element.46), channel_id=1, source_target_pairs={{0,7},{1,0},{8,15},{9,8},{16,23},{17,16},{24,31},{25,24},{32,39},{... | collective-permute-start | bytes 393224 | tf_op jit(solution)/shard_map/ppermute | solution.py:348
  16.8 24.7 %all-to-all-start = ((f32[32,4,8,128]{3,2,1,0:T(8,128)}), f32[32,4,8,128]{3,2,1,0:T(8,128)S(1)}, u32[]{:S(2)}, u32[]{:S(2)}) async-start(f32[32,4,8,128]{3,2,1,0:T(8,128)} %bitcast.24), calls=%async_computation | async-start | bytes 1048576 | tf_op jit(solution)/shard_map/all_to_all | solution.py:353
  24.9 85.0 %all-gather.3.cloned.1.call-start = ((), (), s32[]{:S(2)}) async-start(), calls=%async_computation.5 | async-start | bytes 2359296 | tf_op jit(solution)/shard_map/all_gather | solution.py:357
  25.0 12.5 %collective-permute-start.2 = (f32[64,512]{1,0:T(8,128)S(1)}, f32[64,512]{1,0:T(8,128)S(1)}, u32[]{:S(2)}, u32[]{:S(2)}) collective-permute-start(f32[64,512]{1,0:T(8,128)S(1)} %get-tuple-element.45), channel_id=1, source_target_pairs={{0,6},{1,7},{8,14},{9,15},{16,22},{17,23},{24,30},{25,31},{32,38},... | collective-permute-start | bytes 393224 | tf_op jit(solution)/shard_map/ppermute | solution.py:348
  26.3 14.1 %collective-permute-start.3 = (f32[64,512]{1,0:T(8,128)S(1)}, f32[64,512]{1,0:T(8,128)S(1)}, u32[]{:S(2)}, u32[]{:S(2)}) collective-permute-start(f32[64,512]{1,0:T(8,128)S(1)} %get-tuple-element.44), channel_id=1, source_target_pairs={{0,5},{1,6},{8,13},{9,14},{16,21},{17,22},{24,29},{25,30},{32,37},... | collective-permute-start | bytes 393224 | tf_op jit(solution)/shard_map/ppermute | solution.py:348
  27.6 12.7 %collective-permute-start.4 = (f32[64,512]{1,0:T(8,128)S(1)}, f32[64,512]{1,0:T(8,128)S(1)}, u32[]{:S(2)}, u32[]{:S(2)}) collective-permute-start(f32[64,512]{1,0:T(8,128)S(1)} %get-tuple-element.43), channel_id=1, source_target_pairs={{0,4},{1,5},{8,12},{9,13},{16,20},{17,21},{24,28},{25,29},{32,36},... | collective-permute-start | bytes 393224 | tf_op jit(solution)/shard_map/ppermute | solution.py:348
  28.9 11.4 %collective-permute-start.5 = (f32[64,512]{1,0:T(8,128)S(1)}, f32[64,512]{1,0:T(8,128)S(1)}, u32[]{:S(2)}, u32[]{:S(2)}) collective-permute-start(f32[64,512]{1,0:T(8,128)S(1)} %get-tuple-element.42), channel_id=1, source_target_pairs={{0,3},{1,4},{8,11},{9,12},{16,19},{17,20},{24,27},{25,28},{32,35},... | collective-permute-start | bytes 393224 | tf_op jit(solution)/shard_map/ppermute | solution.py:348
  30.2 10.1 %collective-permute-start.6 = (f32[64,512]{1,0:T(8,128)S(1)}, f32[64,512]{1,0:T(8,128)S(1)}, u32[]{:S(2)}, u32[]{:S(2)}) collective-permute-start(f32[64,512]{1,0:T(8,128)S(1)} %get-tuple-element.41), channel_id=1, source_target_pairs={{0,2},{1,3},{8,10},{9,11},{16,18},{17,19},{24,26},{25,27},{32,34},... | collective-permute-start | bytes 393224 | tf_op jit(solution)/shard_map/ppermute | solution.py:348
  41.5 0.7 copy-start.8
  43.9 15.9 %all-to-all-start.1 = ((f32[32,2,8,128]{3,2,1,0:T(8,128)}), f32[32,2,8,128]{3,2,1,0:T(8,128)S(1)}, u32[]{:S(2)}, u32[]{:S(2)}) async-start(f32[32,2,8,128]{3,2,1,0:T(8,128)} %bitcast.8), calls=%async_computation.1 | async-start | bytes 524288 | tf_op jit(solution)/shard_map/all_to_all | solution.py:361
  51.8 17.4 %collective-permute-start.7 = (f32[64,1024]{1,0:T(8,128)}, f32[64,1024]{1,0:T(8,128)S(1)}, u32[]{:S(2)}, u32[]{:S(2)}) collective-permute-start(f32[64,1024]{1,0:T(8,128)} %copy-done.8), channel_id=1, source_target_pairs={{0,0},{1,16},{2,32},{3,48},{4,64},{5,80},{6,96},{7,112},{8,1},{9,1... | collective-permute-start | bytes 786440 | tf_op jit(solution)/shard_map/ppermute | solution.py:370
  60.4 28.1 %all-to-all-start.2 = ((f32[8,3,8,128]{3,2,1,0:T(8,128)}), f32[8,3,8,128]{3,2,1,0:T(8,128)S(1)}, u32[]{:S(2)}, u32[]{:S(2)}) async-start(f32[8,3,8,128]{3,2,1,0:T(8,128)} %broadcast_in_dim.25), calls=%async_computation.2 | async-start | bytes 196608 | tf_op jit(solution)/shard_map/all_to_all | solution.py:319
  69.2 23.8 %copy-start.9 = (f32[64,1024]{1,0:T(8,128)}, f32[64,1024]{1,0:T(8,128)S(1)}, u32[]{:S(2)}) copy-start(f32[64,1024]{1,0:T(8,128)S(1)} %collective-permute-done.7) | copy-start | bytes 786436
  89.4 10.7 %all-to-all-start.3 = ((f32[16,8,8,128]{3,2,1,0:T(8,128)}), f32[16,8,8,128]{3,2,1,0:T(8,128)S(1)}, u32[]{:S(2)}, u32[]{:S(2)}) async-start(f32[16,8,8,128]{3,2,1,0:T(8,128)} %broadcast_in_dim.27), calls=%async_computation.3 | async-start | bytes 1048576 | tf_op jit(solution)/shard_map/all_to_all | solution.py:319
  92.9 86.0 %all-gather.5.cloned.1.call-start = ((), (), s32[]{:S(2)}) async-start(), calls=%async_computation.6 | async-start | bytes 4456448 | tf_op jit(solution)/shard_map/all_gather | solution.py:376
  100.1 9.8 %collective-permute-start.8 = (f32[16,8,8,128]{3,2,1,0:T(8,128)S(1)}, f32[16,8,8,128]{3,2,1,0:T(8,128)S(1)}, u32[]{:S(2)}, u32[]{:S(2)}) collective-permute-start(f32[16,8,8,128]{3,2,1,0:T(8,128)S(1)} %all-to-all-done.3.own_ref), channel_id=1, source_target_pairs={{0,8},{8,0},{16,24},{24,16},{32,40},{40,32},{48,56},{56,48},{64,72... | collective-permute-start | bytes 1572872 | tf_op jit(solution)/shard_map/ppermute | solution.py:377
  104.3 34.3 %all-to-all-start.4 = ((f32[16,24,8,128]{3,2,1,0:T(8,128)}), f32[16,24,8,128]{3,2,1,0:T(8,128)S(1)}, u32[]{:S(2)}, u32[]{:S(2)}) async-start(f32[16,24,8,128]{3,2,1,0:T(8,128)} %broadcast_in_dim.28), calls=%async_computation.4 | async-start | bytes 3145728 | tf_op jit(solution)/shard_map/all_to_all | solution.py:319
  125.9 1.0 copy-start.6
  138.6 3.9 %collective-permute-start.9 = (f32[16,24,8,128]{3,2,1,0:T(8,128)S(1)}, f32[16,24,8,128]{3,2,1,0:T(8,128)S(1)}, u32[]{:S(2)}, u32[]{:S(2)}) collective-permute-start(f32[16,24,8,128]{3,2,1,0:T(8,128)S(1)} %all-to-all-done.4.own_ref), channel_id=1, source_target_pairs={{0,8},{8,0},{16,24},{24,16},{32,40},{40,32},{48,56},{56,48},{64,72... | collective-permute-start | bytes 4718600 | tf_op jit(solution)/shard_map/ppermute | solution.py:387
  139.5 1.1 copy-start.2
  142.5 1.4 copy-start.3
  143.9 1.0 copy-start.4
  145.0 1.6 copy-start.5
  146.5 1.2 copy-start.7
  178.9 10.6 %collective-permute-start.10 = (f32[1024,1024]{1,0:T(8,128)}, f32[1024,1024]{1,0:T(8,128)S(1)}, u32[]{:S(2)}, u32[]{:S(2)}) collective-permute-start(f32[1024,1024]{1,0:T(8,128)} %all-gather.5.cloned.1.call-done.match_ref), channel_id=1, source_target_pairs={{0,8},{8,0},{16,24},{24,16},{32,40},{40,32},{48,56},{56,48},{64,72... | collective-permute-start | bytes 12582920 | tf_op jit(solution)/shard_map/ppermute | solution.py:393
  179.3 2.2 %copy-start = (f32[512,2048]{1,0:T(8,128)S(1)}, f32[512,2048]{1,0:T(8,128)}, u32[]{:S(2)}) copy-start(f32[512,2048]{1,0:T(8,128)} %gram_ref.3) | copy-start | bytes 12582916
  181.5 2.2 %copy-start.1 = (f32[1024,1024]{1,0:T(8,128)S(1)}, f32[1024,1024]{1,0:T(8,128)}, u32[]{:S(2)}) copy-start(f32[1024,1024]{1,0:T(8,128)} %all-gather.5.cloned.1.call-done.match_ref) | copy-start | bytes 12582916
Sparse Core Ops, SparseCore 0:
  42.3 57.6 all-gather.2
  102.5 67.5 all-gather.4
